TPU v7x, 32 devices: a whole 2x2x4 slice. The times are simulated.
32 devices in a mesh: group: 2 (over x), dp: 16 (over z, y, core).
Axes of the slice: x: 2, y: 2, z: 4, core: 2. Of those that a mesh axis runs over, the one named last changes fastest.
Arguments:
- tokens: bfloat16 [16, 1024, 512], P('dp', 'group'), may hold values from -6 to 6
- qkv_weight: bfloat16 [2, 3, 262144], P(None, None, ('group', 'dp')), may hold values from -0.25 to 0.25
- out_weight: bfloat16 [2, 262144], P(None, ('group', 'dp')), may hold values from -0.75 to 0.75
- ff_weight: bfloat16 [2, 2, 262144], P(None, None, ('group', 'dp')), may hold values from -0.25 to 0.25
- ln_gain: bfloat16 [2, 1024], P(None, ('group', 'dp')), may hold values from 0.5 to 1.5
- ln_bias: bfloat16 [2, 1024], P(None, ('group', 'dp')), may hold values from -2 to 2
- order: int32 [16, 1024], P('dp'), may hold values from 0 to 1023, each once within a row
- cell_lengths: int32 [16, 3], P('dp'), may hold values from 1 to 512, 1024 in all within a row
- known_mask: int32 [16, 512], P('dp'), may hold values 0 or 1
- cotangent: bfloat16 [16, 1024, 512], P('dp', 'group'), may hold values from -6 to 6
Outputs:
- layer_output: float32 [16, 1024, 512], P('dp', 'group')
- input_grad: float32 [16, 1024, 512], P('dp', 'group')
- qkv_grad: float32 [2, 3, 262144], P(None, None, ('group', 'dp'))
- out_proj_grad: float32 [2, 262144], P(None, ('group', 'dp'))
- ff_grad: float32 [2, 2, 262144], P(None, None, ('group', 'dp'))
- gain_grad: float32 [2, 1024], P(None, ('group', 'dp'))
- bias_grad: float32 [2, 1024], P(None, ('group', 'dp'))
Inputs may be any that keep to these rules, and one draw needn't show every extreme that they name: Each row of order holds every position of the row once. `cell_lengths`: a row's cell lengths sum to 1024, the longest is exactly 512.
All inputs are finite; a program needn't handle non-finite values. No bound on the sum of `known_mask` on one device may be relied on, other than what follows from the above.
Results may differ from a plain program's by a relative error of at most 0.019.
Values may be sent and summed in bfloat16 or wider, within the bound.
A program may use at most 128 MiB of HBM per device.

v0:
```python
import math

import jax
import jax.numpy as jnp
from jax import lax
from jax.sharding import PartitionSpec as P

HEADS = 8
FF = 512


def passed_along(value, axis, steps):
    count = lax.axis_size(axis)
    first, last = (max(0, -steps), min(count, count - steps))
    return lax.ppermute(value, axis, [(source, source + steps) for source in range(first, last)])


def layer_norm(values, gain_vec, bias_vec):
    center = values - jnp.mean(values, axis=-1, keepdims=True)
    spread = jnp.mean(center * center, axis=-1, keepdims=True)
    return center * lax.rsqrt(spread + 1e-05) * gain_vec + bias_vec


def shards(
    tokens,
    qkv_weight,
    out_weight,
    ff_weight,
    ln_gain,
    ln_bias,
    order,
    cell_lengths,
    known_mask,
    cotangent,
):
    row_count, half_len, model_width = tokens.shape
    layer_count = qkv_weight.shape[0]
    head_dim = model_width // HEADS
    score_scale = 1.0 / math.sqrt(head_dim)
    token_count = row_count * half_len
    group_index = lax.axis_index("group")
    is_known = group_index == 0
    boundaries = jnp.cumsum(cell_lengths, axis=1)
    cell_of = jnp.sum((boundaries[:, None, :] <= order[:, :, None]).astype(jnp.int32), axis=2)
    key_cell = cell_of[:, :half_len]
    query_cell = lax.dynamic_slice_in_dim(cell_of, group_index * half_len, half_len, 1)
    block_rows = min(512, half_len)
    block_count = half_len // block_rows
    step_list = jnp.arange(row_count * block_count)
    head_shape = (row_count, half_len, HEADS, head_dim)

    def pick_rows(array, row_index):
        whole_row = lax.dynamic_index_in_dim(array, row_index, 0, keepdims=False)
        return whole_row

    def allowed(row_index, start_at):
        query_part = pick_rows(query_cell, row_index)
        key_part = lax.dynamic_index_in_dim(key_cell, row_index, 0, keepdims=False)
        mask_part = lax.dynamic_index_in_dim(known_mask, row_index, 0, keepdims=False)
        same_cell = query_part[:, None] == key_part[None, :]
        diagonal = (start_at + jnp.arange(block_rows))[:, None] == jnp.arange(half_len)[None, :]
        return same_cell & (mask_part[None, :] == 1) & jnp.logical_not(diagonal & is_known)

    def block_scores(step_index, query, key_own, known_key):
        row_index = step_index // block_count
        start_at = step_index % block_count * block_rows
        query_block = pick_rows(query, row_index)
        own_key = pick_rows(key_own, row_index)
        key_rows = lax.dynamic_index_in_dim(known_key, row_index, 0, keepdims=False)
        scores = (
            jnp.einsum("qhd,khd->hqk", query_block, key_rows, preferred_element_type=jnp.float32)
            * score_scale
        )
        scores = jnp.where(allowed(row_index, start_at)[None], scores, -1e30)
        own_score = (
            jnp.einsum("qhd,qhd->hq", query_block, own_key, preferred_element_type=jnp.float32)
            * score_scale
        )
        return (row_index, start_at, query_block, own_key, key_rows, scores, own_score)

    def unpack(pieces):
        qkv_full, out_full, ff_full, gain_full, bias_full = pieces
        qkv = qkv_full.reshape(3, model_width, model_width)
        gains = gain_full.astype(jnp.float32)
        biases = bias_full.astype(jnp.float32)
        return (
            qkv[0],
            qkv[1],
            qkv[2],
            out_full.reshape(model_width, model_width),
            ff_full[0].reshape(model_width, FF),
            ff_full[1].reshape(FF, model_width),
            gains[:model_width],
            gains[model_width:],
            biases[:model_width],
            biases[model_width:],
        )

    def forward_layer(current, params, recompute):
        w_query, w_key, w_value, w_out, w_up, w_down, gain_one, gain_two, bias_one, bias_two = (
            params
        )
        lowered = current.astype(jnp.bfloat16)
        query = (
            jnp.dot(lowered, w_query, preferred_element_type=jnp.float32)
            .astype(jnp.bfloat16)
            .reshape(head_shape)
        )
        key_own = (
            jnp.dot(lowered, w_key, preferred_element_type=jnp.float32)
            .astype(jnp.bfloat16)
            .reshape(head_shape)
        )
        value_own = (
            jnp.dot(lowered, w_value, preferred_element_type=jnp.float32)
            .astype(jnp.bfloat16)
            .reshape(head_shape)
        )
        if recompute:
            received = passed_along((key_own, value_own), "group", 1)
        else:
            received = passed_along((key_own, value_own), "group", 1)
        known_key = jnp.where(is_known, key_own, received[0])
        known_value = jnp.where(is_known, value_own, received[1])

        def attend(step_index):
            row_index, start_at, query_block, own_key, key_rows, scores, own_score = block_scores(
                step_index, query, key_own, known_key
            )
            value_rows = lax.dynamic_index_in_dim(known_value, row_index, 0, keepdims=False)
            own_value = pick_rows(value_own, row_index)
            row_max = jnp.maximum(jnp.max(scores, axis=2), own_score)
            weights = jnp.exp(scores - row_max[:, :, None])
            own_weight = jnp.exp(own_score - row_max)
            row_total = jnp.sum(weights, axis=2) + own_weight
            prob = (weights / row_total[:, :, None]).astype(jnp.bfloat16)
            own_prob = (own_weight / row_total).astype(jnp.bfloat16)
            context = jnp.einsum(
                "hqk,khd->qhd", prob, value_rows, preferred_element_type=jnp.float32
            )
            context = context + own_prob.T[:, :, None].astype(jnp.float32) * own_value.astype(
                jnp.float32
            )
            return (
                context.astype(jnp.bfloat16).reshape(block_rows, model_width),
                row_max + jnp.log(row_total),
            )

        context, log_total = lax.map(attend, step_list)
        context = context.reshape(token_count, model_width)
        branch = jnp.dot(context, w_out, preferred_element_type=jnp.float32)
        first_in = current + branch
        normed = layer_norm(first_in, gain_one, bias_one)
        normed_low = normed.astype(jnp.bfloat16)
        pre_act = jnp.dot(normed_low, w_up, preferred_element_type=jnp.float32)
        hidden = jax.nn.gelu(pre_act).astype(jnp.bfloat16)
        second_in = normed + jnp.dot(hidden, w_down, preferred_element_type=jnp.float32)
        result = layer_norm(second_in, gain_two, bias_two)
        saved = (
            lowered,
            query,
            key_own,
            value_own,
            known_key,
            known_value,
            context,
            log_total,
            first_in,
            normed_low,
            pre_act,
            hidden,
            second_in,
        )
        return (result, saved)

    def backward_attention(
        grad_context, query, key_own, value_own, known_key, known_value, log_total
    ):
        grad_heads = grad_context.reshape(head_shape)

        def attend_back(inputs):
            step_index, total_block = inputs
            row_index, start_at, query_block, own_key, key_rows, scores, own_score = block_scores(
                step_index, query, key_own, known_key
            )
            value_rows = lax.dynamic_index_in_dim(known_value, row_index, 0, keepdims=False)
            own_value = pick_rows(value_own, row_index)
            grad_block = pick_rows(grad_heads, row_index)
            prob = jnp.exp(scores - total_block[:, :, None])
            own_prob = jnp.exp(own_score - total_block)
            grad_prob = jnp.einsum(
                "qhd,khd->hqk", grad_block, value_rows, preferred_element_type=jnp.float32
            )
            grad_own = jnp.sum(
                grad_block.astype(jnp.float32) * own_value.astype(jnp.float32), axis=2
            ).T
            delta = jnp.sum(prob * grad_prob, axis=2) + own_prob * grad_own
            grad_score = (prob * (grad_prob - delta[:, :, None])).astype(jnp.bfloat16)
            grad_own_score = (own_prob * (grad_own - delta)).astype(jnp.bfloat16)
            prob_low = prob.astype(jnp.bfloat16)
            own_low = own_prob.astype(jnp.bfloat16).astype(jnp.float32)
            value_keys = jnp.einsum(
                "hqk,qhd->khd", prob_low, grad_block, preferred_element_type=jnp.float32
            )
            value_self = own_low.T[:, :, None] * grad_block.astype(jnp.float32)
            own_factor = grad_own_score.astype(jnp.float32).T[:, :, None]
            query_grad = jnp.einsum(
                "hqk,khd->qhd", grad_score, key_rows, preferred_element_type=jnp.float32
            )
            query_grad = score_scale * (query_grad + own_factor * own_key.astype(jnp.float32))
            key_keys = score_scale * jnp.einsum(
                "hqk,qhd->khd", grad_score, query_block, preferred_element_type=jnp.float32
            )
            key_self = score_scale * own_factor * query_block.astype(jnp.float32)
            return (query_grad, key_self, value_self, key_keys, value_keys)

        query_grad, key_self, value_self, key_keys, value_keys = lax.map(
            attend_back, (step_list, log_total)
        )
        key_keys = key_keys.reshape((row_count, block_count) + head_shape[1:]).sum(axis=1)
        value_keys = value_keys.reshape((row_count, block_count) + head_shape[1:]).sum(axis=1)
        returned = (
            passed_along(key_keys.astype(jnp.bfloat16), "group", -1).astype(key_keys.dtype),
            passed_along(value_keys.astype(jnp.bfloat16), "group", -1).astype(value_keys.dtype),
        )
        key_grad = key_self + jnp.where(is_known, key_keys + returned[0], 0.0)
        value_grad = value_self + jnp.where(is_known, value_keys + returned[1], 0.0)
        flat = (token_count, model_width)
        return (
            query_grad.reshape(flat).astype(jnp.bfloat16),
            key_grad.reshape(flat).astype(jnp.bfloat16),
            value_grad.reshape(flat).astype(jnp.bfloat16),
        )

    def backward_layer(grad_out, params, saved):
        w_query, w_key, w_value, w_out, w_up, w_down, gain_one, gain_two, bias_one, bias_two = (
            params
        )
        (
            lowered,
            query,
            key_own,
            value_own,
            known_key,
            known_value,
            context,
            log_total,
            first_in,
            normed_low,
            pre_act,
            hidden,
            second_in,
        ) = saved
        _, norm_back = jax.vjp(layer_norm, second_in, gain_two, bias_two)
        grad_second, grad_gain_two, grad_bias_two = norm_back(grad_out)
        grad_ff = grad_second.astype(jnp.bfloat16)
        grad_down = jnp.einsum("nf,nd->fd", hidden, grad_ff, preferred_element_type=jnp.float32)
        grad_hidden = jnp.einsum("nd,fd->nf", grad_ff, w_down, preferred_element_type=jnp.float32)
        _, gelu_back = jax.vjp(jax.nn.gelu, pre_act)
        grad_pre = gelu_back(grad_hidden)[0].astype(jnp.bfloat16)
        grad_up = jnp.einsum("nd,nf->df", normed_low, grad_pre, preferred_element_type=jnp.float32)
        grad_normed = grad_second + jnp.einsum(
            "nf,df->nd", grad_pre, w_up, preferred_element_type=jnp.float32
        )
        _, norm_back = jax.vjp(layer_norm, first_in, gain_one, bias_one)
        grad_first, grad_gain_one, grad_bias_one = norm_back(grad_normed)
        grad_branch = grad_first.astype(jnp.bfloat16)
        grad_wout = jnp.einsum(
            "nc,nd->cd", context, grad_branch, preferred_element_type=jnp.float32
        )
        grad_context = jnp.einsum(
            "nd,cd->nc", grad_branch, w_out, preferred_element_type=jnp.float32
        ).astype(jnp.bfloat16)
        query_grad, key_grad, value_grad = backward_attention(
            grad_context, query, key_own, value_own, known_key, known_value, log_total
        )
        grad_wq = jnp.einsum("nd,ne->de", lowered, query_grad, preferred_element_type=jnp.float32)
        grad_wk = jnp.einsum("nd,ne->de", lowered, key_grad, preferred_element_type=jnp.float32)
        grad_wv = jnp.einsum("nd,ne->de", lowered, value_grad, preferred_element_type=jnp.float32)
        grad_input = grad_first + jnp.einsum(
            "ne,de->nd", query_grad, w_query, preferred_element_type=jnp.float32
        )
        grad_input = grad_input + jnp.einsum(
            "ne,de->nd", key_grad, w_key, preferred_element_type=jnp.float32
        )
        grad_input = grad_input + jnp.einsum(
            "ne,de->nd", value_grad, w_value, preferred_element_type=jnp.float32
        )
        grad_qkv = jnp.stack([grad_wq, grad_wk, grad_wv]).reshape(3, model_width * model_width)
        grad_ffw = jnp.stack([grad_up.reshape(-1), grad_down.reshape(-1)])
        grad_gains = jnp.concatenate([grad_gain_one, grad_gain_two])
        grad_biases = jnp.concatenate([grad_bias_one, grad_bias_two])
        return (grad_input, (grad_qkv, grad_wout.reshape(-1), grad_ffw, grad_gains, grad_biases))

    current = tokens.reshape(token_count, model_width).astype(jnp.float32)
    block_inputs = []
    fetched = []
    for layer_index in range(layer_count):
        params = unpack(
            (
                lax.all_gather(qkv_weight[layer_index], ("group", "dp"), axis=1, tiled=True),
                lax.all_gather(out_weight[layer_index], ("group", "dp"), axis=0, tiled=True),
                lax.all_gather(ff_weight[layer_index], ("group", "dp"), axis=1, tiled=True),
                lax.all_gather(ln_gain[layer_index], ("group", "dp"), axis=0, tiled=True),
                lax.all_gather(ln_bias[layer_index], ("group", "dp"), axis=0, tiled=True),
            )
        )
        fetched.append(params)
        block_inputs.append(current)
        current, _ = forward_layer(current, params, False)
    layer_output = current.reshape(row_count, half_len, model_width)
    grad_current = cotangent.reshape(token_count, model_width).astype(jnp.float32)
    per_layer = [None] * layer_count
    for layer_index in reversed(range(layer_count)):
        params = unpack(
            (
                lax.all_gather(qkv_weight[layer_index], ("group", "dp"), axis=1, tiled=True),
                lax.all_gather(out_weight[layer_index], ("group", "dp"), axis=0, tiled=True),
                lax.all_gather(ff_weight[layer_index], ("group", "dp"), axis=1, tiled=True),
                lax.all_gather(ln_gain[layer_index], ("group", "dp"), axis=0, tiled=True),
                lax.all_gather(ln_bias[layer_index], ("group", "dp"), axis=0, tiled=True),
            )
        )
        _, saved = forward_layer(block_inputs[layer_index], params, True)
        grad_current, layer_terms = backward_layer(grad_current, params, saved)
        per_layer[layer_index] = (
            lax.psum_scatter(layer_terms[0], ("group", "dp"), scatter_dimension=1, tiled=True),
            lax.psum_scatter(layer_terms[1], ("group", "dp"), scatter_dimension=0, tiled=True),
            lax.psum_scatter(layer_terms[2], ("group", "dp"), scatter_dimension=1, tiled=True),
            lax.psum_scatter(layer_terms[3], ("group", "dp"), scatter_dimension=0, tiled=True),
            lax.psum_scatter(layer_terms[4], ("group", "dp"), scatter_dimension=0, tiled=True),
        )
    stacked = tuple(
        (
            jnp.stack([per_layer[layer_index][member] for layer_index in range(layer_count)])
            for member in range(5)
        )
    )
    input_grad = grad_current.reshape(row_count, half_len, model_width)
    return (layer_output, input_grad, stacked[0], stacked[1], stacked[2], stacked[3], stacked[4])


def solution(mesh):
    placed = (
        P("dp", "group", None),
        P(None, None, ("group", "dp")),
        P(None, ("group", "dp")),
        P(None, None, ("group", "dp")),
        P(None, ("group", "dp")),
        P(None, ("group", "dp")),
        P("dp", None),
        P("dp", None),
        P("dp", None),
        P("dp", "group", None),
    )
    return jax.shard_map(
        shards,
        mesh=mesh,
        in_specs=placed,
        out_specs=(
            P("dp", "group", None),
            P("dp", "group", None),
            P(None, None, ("group", "dp")),
            P(None, ("group", "dp")),
            P(None, None, ("group", "dp")),
            P(None, ("group", "dp")),
            P(None, ("group", "dp")),
        ),
        check_vma=False,
    )
```

profile of v0, /device:TPU:0, one launch (start us, length us, event | category | flops | bytes accessed | tf_op | source)
XLA Modules:
  0.0 670.4 jit_solution(10897887178385146527)
XLA Ops:
  7.2 1.5 fusion.123
  8.8 1.8 fusion.122
  15.3 47.1 %all-gather.1 = bf16[1,262144]{1,0:T(2,128)(2,1)S(1)} all-gather(bf16[1,8192]{1,0:T(2,128)(2,1)S(1)} %get-tuple-element.334), channel_id=3, replica_groups=mesh['group'=2,'dp'=16] {'group','dp'}, dimensions={1}, use_global_device_ids=true | all-gather | bytes 540672 | tf_op jit(solution)/shard_map/all_gather | solution.py:302
  62.4 10.9 %reduce.8 = bf16[262144]{0:T(1024)(128)(2,1)S(1)} reduce(bf16[1,262144]{1,0:T(2,128)(2,1)S(1)} %all-gather.1, bf16[]{:T(256)} %constant.389), dimensions={0}, to_apply=%all-gather.1.reduce_sub_computation | reduce | bytes 1048578 | tf_op jit(solution)/shard_map/all_gather | solution.py:302
  73.6 2.3 copy.85
  78.2 37.6 %all-reduce.16 = (bf16[1024]{0:T(1024)(128)(2,1)S(1)}, bf16[1024]{0:T(1024)(128)(2,1)S(1)}, bf16[1024]{0:T(1024)(128)(2,1)S(1)}, bf16[1024]{0:T(1024)(128)(2,1)S(1)}) all-reduce(bf16[1024]{0:T(1024)(128)(2,1)S(1)} %dynamic-update-slice.1, bf16[1024]{0:T(1024)(128)(2,1)S(1)} %dynamic-update-slice, ...), channel_id=5, replica_groups=mesh['group'=2,'dp'=16] {'group','dp'}, use_global_device_ids=true, to_apply=%add.1 | all-reduce | flops 4096 | bytes 16384
  115.8 43.9 %all-gather.6 = bf16[1,262144]{1,0:T(2,128)(2,1)S(1)} all-gather(bf16[1,8192]{1,0:T(2,128)(2,1)S(1)} %get-tuple-element.333), channel_id=8, replica_groups=mesh['group'=2,'dp'=16] {'group','dp'}, dimensions={1}, use_global_device_ids=true | all-gather | bytes 540672 | tf_op jit(solution)/shard_map/all_gather | solution.py:302
  159.6 10.9 %reduce.14 = bf16[262144]{0:T(1024)(128)(2,1)S(1)} reduce(bf16[1,262144]{1,0:T(2,128)(2,1)S(1)} %all-gather.6, bf16[]{:T(256)} %constant.389), dimensions={0}, to_apply=%all-gather.6.reduce_sub_computation | reduce | bytes 1048578 | tf_op jit(solution)/shard_map/all_gather | solution.py:302
  173.0 12.8 %slice_reduce_fusion.6 = (bf16[262144]{0:T(1024)(128)(2,1)S(1)}, bf16[262144]{0:T(1024)(128)(2,1)S(1)}) fusion(bf16[1,2,262144]{2,1,0:T(2,128)(2,1)} %all-gather.17.cloned.1.call-done), kind=kLoop, calls=%fused_computation.117 | loop fusion | bytes 2097152 | tf_op jit(solution)/shard_map/slice | solution.py:91
  187.2 17.2 %slice_reduce_fusion.9 = (bf16[262144]{0:T(1024)(128)(2,1)}, bf16[262144]{0:T(1024)(128)(2,1)S(1)}, bf16[262144]{0:T(1024)(128)(2,1)}) fusion(bf16[1,3,262144]{2,0,1:T(2,128)(2,1)} %all-gather.15.cloned.1.call-done), kind=kLoop, calls=%fused_computation.120 | loop fusion | bytes 3145728 | tf_op jit(solution)/shard_map/slice | solution.py:89
  205.6 1.4 squeeze.197
  207.5 3.8 collective-permute-start.1
  211.2 1.4 squeeze.193
  213.9 2.1 collective-permute-start
  216.0 18.0 %slice_reduce_fusion.4 = (bf16[262144]{0:T(1024)(128)(2,1)}, bf16[262144]{0:T(1024)(128)(2,1)}, bf16[262144]{0:T(1024)(128)(2,1)}) fusion(bf16[1,3,262144]{2,0,1:T(2,128)(2,1)} %all-gather.19.cloned.1.call-done), kind=kLoop, calls=%fused_computation.115 | loop fusion | bytes 3145728 | tf_op jit(solution)/shard_map/slice | solution.py:89
  234.0 2.2 squeeze.207
  236.1 2.2 squeeze.209
  238.3 1.6 fusion.129
  241.2 3.7 fusion.24
  248.8 2.4 fusion.59
  251.2 2.1 collective-permute-start.3
  253.3 13.7 %slice_reduce_fusion.1 = (bf16[262144]{0:T(1024)(128)(2,1)}, bf16[262144]{0:T(1024)(128)(2,1)}) fusion(bf16[1,2,262144]{2,1,0:T(2,128)(2,1)} %all-gather.21.cloned.1.call-done), kind=kLoop, calls=%fused_computation.112 | loop fusion | bytes 2097152 | tf_op jit(solution)/shard_map/slice | solution.py:91
  267.0 2.2 reshape_squeeze.18
  269.1 2.1 reshape_squeeze.19
  271.3 2.2 squeeze.205
  273.4 1.5 convolution_convert_fusion.4
  275.0 1.6 collective-permute-start.2
  276.6 2.8 fusion.132
  280.6 7.5 %collective-permute-done.2 = bf16[1,512,8,64]{1,3,2,0:T(8,128)(2,1)S(1)} collective-permute-done((bf16[1,512,8,64]{1,3,2,0:T(8,128)(2,1)S(1)}, bf16[1,512,8,64]{1,3,2,0:T(8,128)(2,1)S(1)}, u32[]{:S(2)}, u32[]{:S(2)}) %collective-permute-start.2) | collective-permute-done | bytes 524320 | tf_op jit(solution)/shard_map/ppermute | solution.py:15
  288.0 1.5 fusion.23
  292.1 1.6 fusion.30
  296.8 1.4 fusion.6
  298.2 2.4 multiply_reduce_fusion.1
  301.1 2.0 convolution_bitcast_fusion
  305.3 2.6 multiply_convert_fusion.1
  307.9 2.5 convolution_multiply_fusion.1
  314.0 3.1 pad_maximum_fusion.3
  317.1 2.1 fusion.25
  323.1 7.9 %collective-permute-done.4 = bf16[1,512,8,64]{1,3,2,0:T(8,128)(2,1)S(1)} collective-permute-done((bf16[1,512,8,64]{1,3,2,0:T(8,128)(2,1)S(1)}, bf16[1,512,8,64]{1,3,2,0:T(8,128)(2,1)S(1)}, u32[]{:S(2)}, u32[]{:S(2)}) %collective-permute-start.4) | collective-permute-done | bytes 524320 | tf_op jit(solution)/shard_map/ppermute | solution.py:15
  332.7 1.4 fusion.55
  339.2 1.5 fusion.32
  340.8 1.4 fusion.4
  342.2 3.4 multiply_reduce_fusion
  346.6 2.1 copy.155
  348.6 2.1 copy.156
  354.1 2.6 multiply_convert_fusion
  356.7 1.4 convolution_multiply_fusion
  362.5 3.2 pad_maximum_fusion.2
  365.6 4.2 pad_maximum_fusion.1
  371.5 1.5 convolution_bitcast_fusion.11
  372.9 2.6 copy.103
  375.5 3.3 copy.147
  378.8 1.5 fusion.49
  381.1 1.4 convolution_bitcast_fusion.9
  382.5 1.6 copy.105
  384.1 2.1 copy.149
  386.1 1.6 fusion.52
  387.8 1.4 convolution_bitcast_fusion.10
  389.2 1.6 copy.104
  391.8 5.4 pad_maximum_fusion
  398.5 2.6 copy.106
  401.1 42.5 %all-reduce.14 = (f32[1024]{0:T(1024)S(1)}, f32[1024]{0:T(1024)S(1)}, f32[1024]{0:T(1024)S(1)}, f32[1024]{0:T(1024)S(1)}) all-reduce(f32[1024]{0:T(1024)S(1)} %get-tuple-element.376, f32[1024]{0:T(1024)S(1)} %get-tuple-element.378, f32[1024]{0:T(1024)S(1)} %get-tuple-element.377, ...), channel_id=19, replica_groups=mesh['group'=2,'dp'=16] {'group','dp'}, use_global_device_ids=true, to_apply=%region_37.38.clone | all-reduce | flops 4096 | bytes 32768
  445.5 1.7 convolution_add_fusion.1
  449.0 208.7 %all-reduce.19.cloned.1.call-done = (f32[3,262144]{1,0:T(4,128)}, f32[3,262144]{1,0:T(4,128)}, f32[262144]{0:T(1024)}, f32[262144]{0:T(1024)}, f32[2,262144]{1,0:T(2,128)}, /*index=5*/f32[2,262144]{1,0:T(2,128)}) async-done(((f32[3,262144]{1,0:T(4,128)}, f32[3,262144]{1,0:T(4,128)}, f32[262144]{0:T(1024)}, f32[262144]{0:T(1024)}, f32[2,262144]{1,0:T(2,128)}, /*index=5*/f32[2,262144]{1,0:T(2,128)}), ...) | async-done | bytes 12582928
  (245 shorter events, 65.5 us)
Async XLA Ops:
  7.2 164.4 %copy-start.41 = (bf16[1,512,512]{2,1,0:T(8,128)(2,1)S(1)}, bf16[1,512,512]{2,1,0:T(8,128)(2,1)}, u32[]{:S(2)}) copy-start(bf16[1,512,512]{2,1,0:T(8,128)(2,1)} %param.19) | copy-start | bytes 1572868
  7.2 165.8 %all-gather.17.cloned.1.call-start = ((), (), s32[]{:S(2)}) async-start(), calls=%async_computation.1 | async-start | bytes 1081344 | tf_op jit(solution)/shard_map/all_gather | solution.py:303
  8.7 178.5 %all-gather.15.cloned.1.call-start = ((), (), s32[]{:S(2)}) async-start(), calls=%async_computation | async-start | bytes 3244032 | tf_op jit(solution)/shard_map/all_gather | solution.py:301
  10.6 205.4 %all-gather.19.cloned.1.call-start = ((), (), s32[]{:S(2)}) async-start(), calls=%async_computation.2 | async-start | bytes 3244032 | tf_op jit(solution)/shard_map/all_gather | solution.py:301
  11.4 241.9 %all-gather.21.cloned.1.call-start = ((), (), s32[]{:S(2)}) async-start(), calls=%async_computation.3 | async-start | bytes 1081344 | tf_op jit(solution)/shard_map/all_gather | solution.py:303
  11.9 645.7 %all-reduce.19.cloned.1.call-start = ((), (), s32[]{:S(2)}) async-start(), calls=%async_computation.4 | async-start | bytes 29360128
  73.6 171.4 %copy-start.24 = (bf16[512,512]{1,0:T(8,128)(2,1)}, bf16[512,512]{1,0:T(8,128)(2,1)S(1)}, u32[]{:S(2)}) copy-start(bf16[512,512]{1,0:T(8,128)(2,1)S(1)} %reshape.522) | copy-start | bytes 1572868
  73.6 131.1 %copy-start.1 = (bf16[1,512,512]{2,1,0:T(8,128)(2,1)S(1)}, bf16[1,512,512]{2,1,0:T(8,128)(2,1)}, u32[]{:S(2)}) copy-start(bf16[1,512,512]{2,1,0:T(8,128)(2,1)} %param.10) | copy-start | bytes 1572868
  186.1 59.6 %copy-start.12 = (bf16[512,512]{1,0:T(8,128)(2,1)}, bf16[512,512]{1,0:T(8,128)(2,1)S(1)}, u32[]{:S(2)}) copy-start(bf16[512,512]{1,0:T(8,128)(2,1)S(1)} %reshape_squeeze.16) | copy-start | bytes 1572868
  204.7 0.9 copy-start.15
  205.2 34.6 %copy-start.2 = (bf16[512,512]{0,1:T(8,128)(2,1)}, bf16[512,512]{0,1:T(8,128)(2,1)S(1)}, u32[]{:S(2)}) copy-start(bf16[512,512]{0,1:T(8,128)(2,1)S(1)} %convolution_convert_fusion.6) | copy-start | bytes 1572868
  207.0 4.3 copy-start.23
  207.5 32.4 %copy-start.7 = (bf16[512,512]{0,1:T(8,128)(2,1)}, bf16[512,512]{0,1:T(8,128)(2,1)S(1)}, u32[]{:S(2)}) copy-start(bf16[512,512]{0,1:T(8,128)(2,1)S(1)} %get-tuple-element.352) | copy-start | bytes 1572868
  207.5 30.8 %collective-permute-start.1 = (bf16[1,512,8,64]{1,3,2,0:T(8,128)(2,1)S(1)}, bf16[1,512,8,64]{1,3,2,0:T(8,128)(2,1)}, u32[]{:S(2)}, u32[]{:S(2)}) collective-permute-start(bf16[1,512,8,64]{1,3,2,0:T(8,128)(2,1)S(1)} %bitcast.516), channel_id=1, source_target_pairs={{0,16},{1,17},{2,18},{3,19},{4,20},{5,21},{6,22},{7,23},{8,24},{9,... | collective-permute-start | bytes 1572872 | tf_op jit(solution)/shard_map/ppermute | solution.py:15
  212.6 27.3 %copy-start.17 = (bf16[512,512]{1,0:T(8,128)(2,1)}, bf16[512,512]{1,0:T(8,128)(2,1)S(1)}, u32[]{:S(2)}) copy-start(bf16[512,512]{1,0:T(8,128)(2,1)S(1)} %squeeze.193) | copy-start | bytes 1572868
  213.9 27.3 %collective-permute-start = (bf16[1,512,8,64]{1,3,2,0:T(8,128)(2,1)}, bf16[1,512,8,64]{1,3,2,0:T(8,128)(2,1)}, u32[]{:S(2)}, u32[]{:S(2)}) collective-permute-start(bf16[1,512,8,64]{1,3,2,0:T(8,128)(2,1)} %bitcast.5), channel_id=1, source_target_pairs={{0,16},{1,17},{2,18},{3,19},{4,20},{5,21},{6,22},{7,23},{8,24},{9,... | collective-permute-start | bytes 1572872 | tf_op jit(solution)/shard_map/ppermute | solution.py:15
  239.9 5.0 copy-start
  241.2 3.8 copy-start.35
  241.2 5.2 copy-start.42
  244.9 6.3 copy-start.36
  244.9 2.6 copy-start.19
  244.9 3.9 copy-start.33
  246.3 4.9 copy-start.38
  251.2 25.3 %collective-permute-start.3 = (bf16[1,512,8,64]{1,3,2,0:T(8,128)(2,1)}, bf16[1,512,8,64]{1,3,2,0:T(8,128)(2,1)}, u32[]{:S(2)}, u32[]{:S(2)}) collective-permute-start(bf16[1,512,8,64]{1,3,2,0:T(8,128)(2,1)} %bitcast.34), channel_id=1, source_target_pairs={{0,16},{1,17},{2,18},{3,19},{4,20},{5,21},{6,22},{7,23},{8,24},{9,... | collective-permute-start | bytes 1572872 | tf_op jit(solution)/shard_map/ppermute | solution.py:15
  275.0 13.0 %collective-permute-start.2 = (bf16[1,512,8,64]{1,3,2,0:T(8,128)(2,1)S(1)}, bf16[1,512,8,64]{1,3,2,0:T(8,128)(2,1)S(1)}, u32[]{:S(2)}, u32[]{:S(2)}) collective-permute-start(bf16[1,512,8,64]{1,3,2,0:T(8,128)(2,1)S(1)} %bitcast.538), channel_id=1, source_target_pairs={{0,16},{1,17},{2,18},{3,19},{4,20},{5,21},{6,22},{7,23},{8,24},{9,... | collective-permute-start | bytes 1572872 | tf_op jit(solution)/shard_map/ppermute | solution.py:15
  288.0 1.6 copy-start.26
  288.0 2.3 copy-start.32
  288.0 3.0 copy-start.44
  289.6 2.2 copy-start.9
  304.0 28.7 %collective-permute-start.5 = (bf16[1,512,8,64]{1,3,2,0:T(8,128)(2,1)}, bf16[1,512,8,64]{1,3,2,0:T(8,128)(2,1)}, u32[]{:S(2)}, u32[]{:S(2)}) collective-permute-start(bf16[1,512,8,64]{1,3,2,0:T(8,128)(2,1)} %fusion.68), channel_id=1, source_target_pairs={{16,0},{17,1},{18,2},{19,3},{20,4},{21,5},{22,6},{23,7},{24,8},{25... | collective-permute-start | bytes 1572872 | tf_op jit(solution)/shard_map/ppermute | solution.py:15
  307.9 5.0 copy-start.40
  310.5 20.5 %collective-permute-start.4 = (bf16[1,512,8,64]{1,3,2,0:T(8,128)(2,1)S(1)}, bf16[1,512,8,64]{1,3,2,0:T(8,128)(2,1)S(1)}, u32[]{:S(2)}, u32[]{:S(2)}) collective-permute-start(bf16[1,512,8,64]{1,3,2,0:T(8,128)(2,1)S(1)} %fusion.67), channel_id=1, source_target_pairs={{16,0},{17,1},{18,2},{19,3},{20,4},{21,5},{22,6},{23,7},{24,8},{25... | collective-permute-start | bytes 1572872 | tf_op jit(solution)/shard_map/ppermute | solution.py:15
  317.1 5.5 copy-start.20
  319.2 13.1 %copy-start.34 = (bf16[512,512]{1,0:T(8,128)(2,1)S(1)}, bf16[512,512]{1,0:T(8,128)(2,1)}, u32[]{:S(2)}) copy-start(bf16[512,512]{1,0:T(8,128)(2,1)} %squeeze.209) | copy-start | bytes 1572868
  321.0 13.1 %copy-start.14 = (bf16[512,512]{1,0:T(8,128)(2,1)S(1)}, bf16[512,512]{1,0:T(8,128)(2,1)}, u32[]{:S(2)}) copy-start(bf16[512,512]{1,0:T(8,128)(2,1)} %squeeze.205) | copy-start | bytes 1572868
  323.0 12.2 %copy-start.39 = (f32[512,512]{1,0:T(8,128)S(1)}, f32[512,512]{1,0:T(8,128)}, u32[]{:S(2)}) copy-start(f32[512,512]{1,0:T(8,128)} %copy-done.38) | copy-start | bytes 3145732
  323.1 12.2 %copy-start.43 = (bf16[512,512]{1,0:T(8,128)(2,1)S(1)}, bf16[512,512]{1,0:T(8,128)(2,1)}, u32[]{:S(2)}) copy-start(bf16[512,512]{1,0:T(8,128)(2,1)} %reshape_squeeze.17) | copy-start | bytes 1572868
  332.7 3.6 copy-start.13
  336.3 2.4 copy-start.37
  336.3 2.9 copy-start.25
  336.3 4.4 slice-start
  337.7 3.1 slice-start.1
  340.7 13.4 %copy-start.11 = (bf16[512,512]{0,1:T(8,128)(2,1)}, bf16[512,512]{0,1:T(8,128)(2,1)S(1)}, u32[]{:S(2)}) copy-start(bf16[512,512]{0,1:T(8,128)(2,1)S(1)} %get-tuple-element.375) | copy-start | bytes 1572868
  342.2 9.8 %copy-start.4 = (f32[8,64,512]{2,1,0:T(8,128)}, f32[8,64,512]{2,1,0:T(8,128)S(1)}, u32[]{:S(2)}) copy-start(f32[8,64,512]{2,1,0:T(8,128)S(1)} %fusion.4) | copy-start | bytes 3145732
  352.8 26.0 %collective-permute-start.7 = (bf16[1,512,8,64]{1,3,2,0:T(8,128)(2,1)}, bf16[1,512,8,64]{1,3,2,0:T(8,128)(2,1)}, u32[]{:S(2)}, u32[]{:S(2)}) collective-permute-start(bf16[1,512,8,64]{1,3,2,0:T(8,128)(2,1)} %fusion.70), channel_id=1, source_target_pairs={{16,0},{17,1},{18,2},{19,3},{20,4},{21,5},{22,6},{23,7},{24,8},{25... | collective-permute-start | bytes 1572872 | tf_op jit(solution)/shard_map/ppermute | solution.py:15
  354.1 2.6 copy-start.3
  356.7 5.7 copy-start.30
  356.7 5.7 copy-start.31
  358.1 7.5 %copy-start.6 = (f32[8,64,512]{2,1,0:T(8,128)}, f32[8,64,512]{2,1,0:T(8,128)S(1)}, u32[]{:S(2)}) copy-start(f32[8,64,512]{2,1,0:T(8,128)S(1)} %convolution_multiply_fusion) | copy-start | bytes 3145732
  358.1 11.7 %copy-start.8 = (bf16[512,512]{0,1:T(8,128)(2,1)S(1)}, bf16[512,512]{0,1:T(8,128)(2,1)}, u32[]{:S(2)}) copy-start(bf16[512,512]{0,1:T(8,128)(2,1)} %copy-done.7) | copy-start | bytes 1572868
  359.0 27.1 %collective-permute-start.6 = (bf16[1,512,8,64]{1,3,2,0:T(8,128)(2,1)}, bf16[1,512,8,64]{1,3,2,0:T(8,128)(2,1)}, u32[]{:S(2)}, u32[]{:S(2)}) collective-permute-start(bf16[1,512,8,64]{1,3,2,0:T(8,128)(2,1)} %fusion.69), channel_id=1, source_target_pairs={{16,0},{17,1},{18,2},{19,3},{20,4},{21,5},{22,6},{23,7},{24,8},{25... | collective-permute-start | bytes 1572872 | tf_op jit(solution)/shard_map/ppermute | solution.py:15
  365.6 13.2 %copy-start.5 = (f32[8,64,512]{2,1,0:T(8,128)S(1)}, f32[8,64,512]{2,1,0:T(8,128)}, u32[]{:S(2)}) copy-start(f32[8,64,512]{2,1,0:T(8,128)} %copy-done.4) | copy-start | bytes 3145732
  370.7 0.8 copy-start.21
  380.3 0.8 copy-start.27
  387.8 9.5 %copy-start.29 = (bf16[1,512,8,64]{1,3,2,0:T(8,128)(2,1)}, bf16[1,512,8,64]{1,3,2,0:T(8,128)(2,1)S(1)}, u32[]{:S(2)}) copy-start(bf16[1,512,8,64]{1,3,2,0:T(8,128)(2,1)S(1)} %fusion.52) | copy-start | bytes 1572868
  397.3 1.0 copy-start.10
  397.3 47.8 %copy-start.16 = (bf16[512,512]{1,0:T(8,128)(2,1)S(1)}, bf16[512,512]{1,0:T(8,128)(2,1)}, u32[]{:S(2)}) copy-start(bf16[512,512]{1,0:T(8,128)(2,1)} %copy-done.15) | copy-start | bytes 1572868
  397.3 47.8 %copy-start.22 = (bf16[512,8,64]{0,2,1:T(8,128)(2,1)S(1)}, bf16[512,8,64]{0,2,1:T(8,128)(2,1)}, u32[]{:S(2)}) copy-start(bf16[512,8,64]{0,2,1:T(8,128)(2,1)} %copy-done.21) | copy-start | bytes 1572868
  397.3 49.9 %copy-start.18 = (bf16[512,512]{1,0:T(8,128)(2,1)S(1)}, bf16[512,512]{1,0:T(8,128)(2,1)}, u32[]{:S(2)}) copy-start(bf16[512,512]{1,0:T(8,128)(2,1)} %copy-done.17) | copy-start | bytes 1572868
  398.5 48.7 %copy-start.28 = (bf16[1,512,8,64]{1,3,2,0:T(8,128)(2,1)S(1)}, bf16[1,512,8,64]{1,3,2,0:T(8,128)(2,1)}, u32[]{:S(2)}) copy-start(bf16[1,512,8,64]{1,3,2,0:T(8,128)(2,1)} %copy-done.27) | copy-start | bytes 1572868
Sparse Core Ops, SparseCore 0:
  11.5 56.6 all-gather.16
  71.7 58.6 all-gather.14
  133.9 58.5 all-gather.18
  195.2 53.2 all-gather.20
  397.4 260.1 all-reduce.18
where the time goes:
time: 678 us; the launch traced here: 670 us
  waiting for transfers between devices  225 us (33%)
  blocking collectives  171 us (25%)
  local copies, waits for them, and re-layouts  124 us (18%)
  other arithmetic  62.8 us (9%)
  matrix products  57 us (8%)
  between operations  15.5 us (2%)
  starting transfers between devices  14.8 us (2%)
    unnamed x6, waiting for transfers between devices  210 us
    all_gather x2, blocking collectives, shards(): lax.all_gather(out_weight[layer_index], ('group', 'dp'), axis=0, tiled=True)  90.9 us
    unnamed x2, blocking collectives  80.1 us
    slice x2, local copies, waits for them, and re-layouts, unpack(): qkv[2]  35.2 us
    unnamed x123, local copies, waits for them, and re-layouts  33.5 us
    slice x2, local copies, waits for them, and re-layouts, unpack(): ff_full[0].reshape(model_width, FF)  26.4 us
    all_gather x2, other arithmetic, shards(): lax.all_gather(out_weight[layer_index], ('group', 'dp'), axis=0, tiled=True)  21.8 us
    ppermute x8, waiting for transfers between devices, passed_along(): lax.ppermute(value, axis, [(source, source + steps) for source in range(f...  15.3 us
  transfers between devices with their start and end apart: 13, of which 3 were waited for; matrix products, arithmetic and copies ran while one was open for 28% of the time, Pallas kernels for 0%

commit v1 on v0

v1 whole, which is shorter than its diff:
```python
import functools
import math

import jax
import jax.numpy as jnp
from jax import lax
from jax.experimental import pallas as pl
from jax.experimental.pallas import tpu as pltpu
from jax.sharding import PartitionSpec as P

HEADS = 8
BLOCKS = 32
ZS = 4
MESH = pl.DeviceIdType.MESH
F32 = jnp.float32
BF16 = jnp.bfloat16

KEY, VALUE, QUERY, OUT, UP, DOWN = range(6)
VECTORS = 6
MATRICES = 13
GATHERS = ((0, 1), (1, 2), (2, 3), (3, 7), (7, 10), (10, 13))
REDUCES = ((9, 12), (6, 9), (3, 6), (0, 3))


def dot(left, right, left_dim, right_dim):
    return lax.dot_general(
        left, right, (((left_dim,), (right_dim,)), ((), ())), preferred_element_type=F32
    )


def kernel(replicas, *refs):
    (
        tok_ref, cot_ref, shard_ref, order_ref, length_ref, known_ref,
        out_ref, inp_ref, grad_ref, vec_ref,
        w, x_in, cot, meta_own, meta, bias, cur, low, qs, ks, vs, kk, kv, probs, own_p,
        ctx, xhat1, r1, normed_low, pre, hidden, xhat2, r2, work, dctx, dq, dkk, dvv,
        send_k, send_v, got_k, got_v,
        g_buf, rc, r2a, r2b, r3, r4, vec_sum, vec_got,
        swap_s, swap_r, ag_s, ag_r, kv_s, kv_r, dkv_s, dkv_r, rs_s, rs_r, vs_s, vs_r,
    ) = refs
    n, d = tok_ref.shape
    hd = d // HEADS
    pairs = d // 128
    scale = 1.0 / math.sqrt(hd)
    gi = lax.axis_index("group")
    dp = lax.axis_index("dp")
    hi, lo = dp // replicas, dp % replicas
    z, y, c = hi // 4, (hi // 2) % 2, hi % 2
    half = dp % 2

    def place(g_, z_, y_, c_):
        return (g_, (z_ * 4 + y_ * 2 + c_) * replicas + lo)

    other_x = place(1 - gi, z, y, c)
    other_y = place(gi, z, 1 - y, c)
    other_c = place(gi, z, y, 1 - c)
    others_z = [place(gi, (z + i) % ZS, y, c) for i in range(1, ZS)]
    sibling = (gi, dp + 1 - 2 * half)
    partner = (1 - gi, dp + 1 - 2 * half)
    is_known = half == 0
    swaps = gi != half

    partners = [other_x, other_y, other_c, partner] + others_z
    if replicas > 1:
        partners.append(sibling)
    barrier = pltpu.get_barrier_semaphore()
    for device in partners:
        pl.semaphore_signal(barrier, inc=1, device_id=device, device_id_type=MESH)

    def remote(src, dst, send, recv, device):
        return pltpu.make_async_remote_copy(
            src_ref=src, dst_ref=dst, send_sem=send, recv_sem=recv, device_id=device, device_id_type=MESH
        )

    def ag_copies(s, phase):
        a, b = GATHERS[s]
        m = pl.ds(a, b - a)
        if phase == 0:
            block = w.at[m, gi, z, y, c]
            plan = [(block, dev) for dev in others_z]
            base = 0
        elif phase == 1:
            plan = [
                (w.at[m, gi, :, y, c, :, pl.ds(0, d // 2)], other_x),
                (w.at[m, gi, :, y, c, :, pl.ds(d // 2, d // 2)], other_y),
            ]
            base = 3
        elif phase == 2:
            plan = [
                (w.at[m, :, :, y, c, :, pl.ds(0, d // 2)], other_y),
                (w.at[m, gi, :, :, c, :, pl.ds(d // 2, d // 2)], other_x),
            ]
            base = 5
        else:
            plan = [(w.at[m, :, :, :, c], other_c)]
            base = 7
        return [remote(r, r, ag_s.at[s, base + i], ag_r.at[s, base + i], dev) for i, (r, dev) in enumerate(plan)]

    def ag_start(s, phase):
        for copy in ag_copies(s, phase):
            copy.start()

    def ag_wait(s, phase):
        for copy in ag_copies(s, phase):
            copy.wait()

    def ag_step(s, phase):
        ag_wait(s, phase - 1)
        ag_start(s, phase)

    def rs_copies(s, phase):
        a, b = REDUCES[s]
        m = pl.ds(a, b - a)
        h0, h1 = pl.ds(0, d // 2), pl.ds(d // 2, d // 2)
        if phase == 0:
            plan = [(g_buf.at[m, :, :, :, 1 - c], rc.at[m], other_c)]
            base = 0
        elif phase == 1:
            plan = [
                (rc.at[m, :, :, 1 - y, :, h0], r2a.at[m], other_y),
                (rc.at[m, 1 - gi, :, :, :, h1], r2b.at[m], other_x),
            ]
            base = 1
        elif phase == 2:
            plan = [
                (r2a.at[m, 1 - gi], r3.at[m, :, :, h0], other_x),
                (r2b.at[m, :, 1 - y], r3.at[m, :, :, h1], other_y),
            ]
            base = 3
        else:
            plan = [(r3.at[m, (z + i) % ZS], r4.at[i - 1, m], others_z[i - 1]) for i in range(1, ZS)]
            base = 5
        return [remote(a_, b_, rs_s.at[s, base + i], rs_r.at[s, base + i], dev) for i, (a_, b_, dev) in enumerate(plan)]

    def rs_start(s, phase):
        for copy in rs_copies(s, phase):
            copy.start()

    def rs_wait(s, phase):
        for copy in rs_copies(s, phase):
            copy.wait()

    def rs_add(s, phase):
        a, b = REDUCES[s]
        h0, h1 = slice(0, d // 2), slice(d // 2, d)
        for m in range(a, b):
            if phase == 0:
                rc[m] = (rc[m].astype(F32) + g_buf[m, :, :, :, c].astype(F32)).astype(BF16)
            elif phase == 1:
                r2a[m] = (r2a[m].astype(F32) + rc[m, :, :, y, :, h0].astype(F32)).astype(BF16)
                r2b[m] = (r2b[m].astype(F32) + rc[m, gi, :, :, :, h1].astype(F32)).astype(BF16)
            elif phase == 2:
                r3[m, :, :, h0] = (r3[m, :, :, h0].astype(F32) + r2a[m, gi].astype(F32)).astype(BF16)
                r3[m, :, :, h1] = (r3[m, :, :, h1].astype(F32) + r2b[m, :, y].astype(F32)).astype(BF16)
            else:
                total = r3[m, z].astype(F32)
                for i in range(ZS - 1):
                    total = total + r4[i, m].astype(F32)
                grad_ref[m] = total

    def rs_step(s, phase):
        rs_wait(s, phase - 1)
        rs_add(s, phase - 1)
        if phase < 4:
            rs_start(s, phase)

    def vec_copies(phase):
        if phase == 3:
            return [
                remote(vec_sum.at[3], vec_got.at[2 + i], vs_s.at[2 + i], vs_r.at[2 + i], others_z[i - 1])
                for i in range(1, ZS)
            ]
        device = (other_c, other_y, other_x)[phase]
        return [remote(vec_sum.at[phase], vec_got.at[phase], vs_s.at[phase], vs_r.at[phase], device)]

    def vec_start(phase):
        for copy in vec_copies(phase):
            copy.start()

    def vec_step(phase):
        for copy in vec_copies(phase - 1):
            copy.wait()
        if phase < 4:
            vec_sum[phase] = vec_sum[phase - 1] + vec_got[phase - 1]
            vec_start(phase)

    def swap_copy(index, src, dst):
        return remote(src, dst, swap_s.at[index], swap_r.at[index], partner)

    w[:, gi, z, y, c] = shard_ref[...]
    position = order_ref[...]
    cell = jnp.zeros(position.shape, jnp.int32)
    edge = jnp.zeros((1, 1), jnp.int32)
    for i in range(length_ref.shape[1]):
        edge = edge + length_ref[:, i : i + 1]
        cell = cell + (edge <= position).astype(jnp.int32)
    meta_own[0:1, :] = cell.astype(F32)
    meta_own[1:2, 0:n] = known_ref[...].astype(F32)

    pl.semaphore_wait(barrier, len(partners))
    for s in range(4):
        ag_start(s, 0)

    @pl.when(swaps)
    def _():
        swap_copy(0, meta_own, meta).start()
        swap_copy(1, tok_ref, x_in).start()

    @pl.when(jnp.logical_not(swaps))
    def _():
        meta[...] = meta_own[...]
        x_in[...] = tok_ref[...]
        cot[...] = cot_ref[...]

    ag_step(0, 1)
    ag_step(1, 1)
    ag_step(0, 2)
    ag_step(2, 1)
    ag_step(1, 2)
    ag_step(0, 3)

    lane = lax.broadcasted_iota(jnp.int32, (HEADS, d), 1)
    head_of = (lane // hd == lax.broadcasted_iota(jnp.int32, (HEADS, d), 0)).astype(BF16)

    def head_sum(product):
        high = product.astype(BF16)
        rest = (product - high.astype(F32)).astype(BF16)
        return dot(head_of, high, 1, 1) + dot(head_of, rest, 1, 1)

    def weight(i):
        return w[i].reshape(d, d)

    @pl.when(swaps)
    def _():
        swap_copy(0, meta_own, meta).wait()

    kinds = lax.broadcasted_iota(jnp.int32, (HEADS, n), 0).astype(F32)
    query_cell = jnp.where(is_known, meta[0:1, 0:n], meta[0:1, n : 2 * n])
    query_code = (kinds == query_cell).astype(BF16)
    key_code = ((kinds == meta[0:1, 0:n]) & (meta[1:2, 0:n] == 1.0)).astype(BF16)
    same = dot(key_code, query_code, 0, 0)
    key_at = lax.broadcasted_iota(jnp.int32, (n, n), 0)
    query_at = lax.broadcasted_iota(jnp.int32, (n, n), 1) + half * 2 * n
    bias[...] = jnp.where((same > 0.5) & (key_at != query_at), 0.0, -1e30)

    ag_step(2, 2)
    ag_step(1, 3)
    ag_step(3, 1)
    ag_step(2, 3)

    @pl.when(swaps)
    def _():
        swap_copy(1, tok_ref, x_in).wait()
        swap_copy(2, cot_ref, cot).start()

    cur[...] = x_in[...].astype(F32)

    def in_head(h, value):
        at = lax.broadcasted_iota(jnp.int32, value.shape, 1)
        return jnp.where(at // hd == h, value, jnp.zeros_like(value))

    def pair_lanes(i):
        return pl.ds(pl.multiple_of(i * 128, 128), 128)

    def kv_copies(l):
        return [
            remote(kk.at[l], kk.at[l], kv_s.at[l, 0], kv_r.at[l, 0], sibling),
            remote(kv.at[l], kv.at[l], kv_s.at[l, 1], kv_r.at[l, 1], sibling),
        ]

    def attend(l, first, last):
        def body(i, carry):
            lanes = pair_lanes(i)
            k_pair, v_pair, q_pair = kk[l, :, lanes], kv[l, :, lanes], qs[l, :, lanes]
            total_ctx = jnp.zeros((n, 128), F32)
            for h in range(2):
                own = own_p[l, pl.ds(i * 2 + h, 1), :]
                scores = dot(in_head(h, k_pair), q_pair, 1, 1) + bias[...]
                top = jnp.maximum(jnp.max(scores, axis=0, keepdims=True), own)
                weights = jnp.exp(scores - top)
                own_weight = jnp.exp(own - top)
                inverse = 1.0 / (jnp.sum(weights, axis=0, keepdims=True) + own_weight)
                prob = (weights * inverse).astype(BF16)
                probs[l, i * 2 + h] = prob
                own_p[l, pl.ds(i * 2 + h, 1), :] = (own_weight * inverse).astype(BF16).astype(F32)
                total_ctx = total_ctx + dot(prob, in_head(h, v_pair), 0, 0)
            work[:, lanes] = total_ctx
            return carry

        lax.fori_loop(first, last, body, 0)

    def norm(values, gain, shift, xhat, spread):
        center = values - jnp.mean(values, axis=1, keepdims=True)
        r = lax.rsqrt(jnp.mean(center * center, axis=1, keepdims=True) + 1e-05)
        hat = center * r
        xhat[...] = hat.astype(BF16)
        spread[...] = r
        return hat * gain + shift

    def vectors(l):
        blocks = w[VECTORS, :, :, :, :, :, 0:128].reshape(BLOCKS, 16, 128)
        rows = jnp.sum(blocks.astype(F32), axis=1).astype(BF16)
        wide = 2 * d
        per = wide // BLOCKS
        source = lax.broadcasted_iota(jnp.int32, (128, wide), 0)
        target = lax.broadcasted_iota(jnp.int32, (128, wide), 1)
        owner = lax.broadcasted_iota(jnp.int32, (BLOCKS, wide), 0)
        column = lax.broadcasted_iota(jnp.int32, (BLOCKS, wide), 1)
        found = []
        for which in range(2):
            pick = (source == target % per + (l * 2 + which) * per).astype(BF16)
            spread_out = dot(rows, pick, 1, 0)
            found.append(jnp.sum(jnp.where(column // per == owner, spread_out, 0.0), axis=0, keepdims=True))
        gains, shifts = found
        return gains[:, :d], shifts[:, :d], gains[:, d:], shifts[:, d:]

    def forward(l, first_point, mid_point, late_point, chunks):
        base = l * 7
        low[l] = cur[...].astype(BF16)
        if chunks[0] is not None:
            ag_wait(chunks[0], 3)
        ks[l] = dot(low[l], weight(base + KEY), 1, 0).astype(BF16)

        @pl.when(is_known)
        def _():
            kk[l] = ks[l]
            kv_copies(l)[0].start()

        if chunks[1] is not None:
            ag_wait(chunks[1], 3)
        vs[l] = dot(low[l], weight(base + VALUE), 1, 0).astype(BF16)

        @pl.when(is_known)
        def _():
            kv[l] = vs[l]
            kv_copies(l)[1].start()

        if chunks[2] is not None:
            ag_wait(chunks[2], 3)
        qs[l] = (dot(low[l], weight(base + QUERY), 1, 0).astype(BF16).astype(F32) * scale).astype(BF16)
        own_p[l] = head_sum(qs[l].astype(F32) * ks[l].astype(F32))
        first_point()

        @pl.when(jnp.logical_not(is_known))
        def _():
            for copy in kv_copies(l):
                copy.wait_recv()

        attend(l, 0, pairs // 2)
        mid_point()
        attend(l, pairs // 2, pairs)
        spread_own = dot(own_p[l].astype(BF16), head_of, 0, 0)
        ctx[l] = (work[...] + spread_own * vs[l].astype(F32)).astype(BF16)
        late_point()
        gain1, shift1, gain2, shift2 = vectors(l)
        first_in = cur[...] + dot(ctx[l], weight(base + OUT), 1, 0)
        normed = norm(first_in, gain1, shift1, xhat1.at[l], r1.at[l])
        work[...] = normed
        normed_low[l] = normed.astype(BF16)
        pre_act = dot(normed_low[l], weight(base + UP), 1, 0)
        pre[l] = pre_act
        hidden[l] = jax.nn.gelu(pre_act).astype(BF16)
        second_in = work[...] + dot(hidden[l], weight(base + DOWN), 1, 0)
        cur[...] = norm(second_in, gain2, shift2, xhat2.at[l], r2.at[l])

    def first0():
        ag_step(3, 2)
        ag_start(4, 0)
        ag_start(5, 0)

    def mid0():
        ag_step(3, 3)
        ag_step(4, 1)
        ag_step(5, 1)

    def late0():
        ag_wait(3, 3)
        ag_step(4, 2)
        ag_step(5, 2)

    forward(0, first0, mid0, late0, (0, 1, 2))
    ag_step(4, 3)
    ag_wait(4, 3)

    def mid1():
        ag_step(5, 3)

    def late1():
        ag_wait(5, 3)

    forward(1, lambda: None, mid1, late1, (None, None, None))
    x_in[...] = cur[...].astype(BF16)

    @pl.when(swaps)
    def _():
        swap_copy(3, x_in, out_ref).start()
        swap_copy(2, cot_ref, cot).wait()

    @pl.when(jnp.logical_not(swaps))
    def _():
        out_ref[...] = x_in[...]

    cur[...] = cot[...].astype(F32)

    def norm_back(grad, gain, xhat, spread):
        hat = xhat[...].astype(F32)
        e = grad * gain
        mean_e = jnp.mean(e, axis=1, keepdims=True)
        mean_eh = jnp.mean(e * hat, axis=1, keepdims=True)
        out = spread[...] * (e - mean_e - hat * mean_eh)
        return out, jnp.sum(grad * hat, axis=0, keepdims=True), jnp.sum(grad, axis=0, keepdims=True)

    def dkv_copies(l, i):
        lanes = pair_lanes(i)
        return [
            remote(send_k.at[l, :, lanes], got_k.at[l, :, lanes], dkv_s.at[l, i, 0], dkv_r.at[l, i, 0], sibling),
            remote(send_v.at[l, :, lanes], got_v.at[l, :, lanes], dkv_s.at[l, i, 1], dkv_r.at[l, i, 1], sibling),
        ]

    def store_grad(index, value):
        g_buf[index] = value.astype(BF16).reshape(g_buf.shape[1:])

    def backward(l, start_point, ff_point, attn_point, mid_point, end_point):
        base, gbase = l * 7, l * 6
        gain1, shift1, gain2, shift2 = vectors(l)
        grad_second, grad_gain2, grad_shift2 = norm_back(cur[...], gain2, xhat2.at[l], r2.at[l])
        work[...] = grad_second
        grad_ff = grad_second.astype(BF16)
        store_grad(gbase + DOWN, dot(hidden[l], grad_ff, 0, 0))
        start_point()
        grad_hidden = dot(grad_ff, weight(base + DOWN), 1, 1)
        act = pre[l]
        coef = math.sqrt(2.0 / math.pi)
        tanh = jnp.tanh(coef * (act + 0.044715 * act * act * act))
        slope = 0.5 * (1.0 + tanh) + 0.5 * act * (1.0 - tanh * tanh) * coef * (1.0 + 3 * 0.044715 * act * act)
        grad_pre = (grad_hidden * slope).astype(BF16)
        store_grad(gbase + UP, dot(normed_low[l], grad_pre, 0, 0))
        grad_normed = work[...] + dot(grad_pre, weight(base + UP), 1, 1)
        ff_point()
        grad_first, grad_gain1, grad_shift1 = norm_back(grad_normed, gain1, xhat1.at[l], r1.at[l])
        cur[...] = grad_first
        grad_branch = grad_first.astype(BF16)
        vec_sum[0, l * 4 : l * 4 + 1, 0:d] = grad_gain1
        vec_sum[0, l * 4 : l * 4 + 1, d : 2 * d] = grad_gain2
        vec_sum[0, l * 4 + 1 : l * 4 + 2, 0:d] = grad_shift1
        vec_sum[0, l * 4 + 1 : l * 4 + 2, d : 2 * d] = grad_shift2
        store_grad(gbase + OUT, dot(ctx[l], grad_branch, 0, 0))
        dctx[...] = dot(grad_branch, weight(base + OUT), 1, 1).astype(BF16)
        wide_grad = dctx[...].astype(F32)
        delta = head_sum(wide_grad * ctx[l].astype(F32))
        own_grad = head_sum(wide_grad * vs[l].astype(F32))
        own_score_grad = (own_p[l] * (own_grad - delta)).astype(BF16)
        work[0:HEADS, :] = delta
        attn_point()

        def body(i, carry):
            lanes = pair_lanes(i)
            k_pair, v_pair, q_pair = kk[l, :, lanes], kv[l, :, lanes], qs[l, :, lanes]
            c_pair = dctx[:, lanes]
            sum_q = jnp.zeros((n, 128), F32)
            sum_k = jnp.zeros((n, 128), F32)
            sum_v = jnp.zeros((n, 128), F32)
            for h in range(2):
                prob = probs[l, i * 2 + h]
                grad_prob = dot(in_head(h, v_pair), c_pair, 1, 1)
                shift = work[pl.ds(i * 2 + h, 1), :]
                grad_score = (prob.astype(F32) * (grad_prob - shift)).astype(BF16)
                sum_v = sum_v + dot(prob, in_head(h, c_pair), 1, 0)
                sum_k = sum_k + dot(grad_score, in_head(h, q_pair), 1, 0)
                sum_q = sum_q + dot(grad_score, in_head(h, k_pair), 0, 0)
            dq[:, lanes] = sum_q

            @pl.when(is_known)
            def _():
                dkk[:, lanes] = sum_k
                dvv[:, lanes] = sum_v

            @pl.when(jnp.logical_not(is_known))
            def _():
                send_k[l, :, lanes] = sum_k.astype(BF16)
                send_v[l, :, lanes] = sum_v.astype(BF16)
                for copy in dkv_copies(l, i):
                    copy.start()

            return carry

        lax.fori_loop(0, pairs // 2, body, 0)
        mid_point()
        lax.fori_loop(pairs // 2, pairs, body, 0)
        own_wide = dot(own_score_grad, head_of, 0, 0)
        p_wide = dot(own_p[l].astype(BF16), head_of, 0, 0)
        query_grad = (scale * (dq[...] + own_wide * ks[l].astype(F32))).astype(BF16)
        store_grad(gbase + QUERY, dot(low[l], query_grad, 0, 0))
        cur[...] += dot(query_grad, weight(base + QUERY), 1, 1)
        own_k = own_wide * qs[l].astype(F32)
        own_v = p_wide * dctx[...].astype(F32)

        @pl.when(is_known)
        def _():
            for i in range(pairs):
                for copy in dkv_copies(l, i):
                    copy.wait_recv()
            dkk[...] = dkk[...] + got_k[l].astype(F32) + own_k
            dvv[...] = dvv[...] + got_v[l].astype(F32) + own_v

        @pl.when(jnp.logical_not(is_known))
        def _():
            dkk[...] = own_k
            dvv[...] = own_v

        key_grad = dkk[...].astype(BF16)
        value_grad = dvv[...].astype(BF16)
        store_grad(gbase + KEY, dot(low[l], key_grad, 0, 0))
        store_grad(gbase + VALUE, dot(low[l], value_grad, 0, 0))
        end_point()
        cur[...] += dot(key_grad, weight(base + KEY), 1, 1) + dot(value_grad, weight(base + VALUE), 1, 1)

    vec_sum[0] = jnp.zeros(vec_sum.shape[1:], F32)

    backward(1, lambda: None, lambda: None, lambda: rs_start(0, 0), lambda: rs_step(0, 1), lambda: rs_start(1, 0))

    def start0():
        rs_step(0, 2)
        rs_step(1, 1)

    def ff0():
        rs_step(0, 3)

    def attn0():
        rs_step(1, 2)
        rs_start(2, 0)
        vec_start(0)

    def mid0b():
        rs_step(0, 4)
        rs_step(1, 3)
        rs_step(2, 1)
        vec_step(1)

    def end0():
        rs_start(3, 0)
        rs_step(2, 2)
        vec_step(2)
        rs_step(1, 4)

    backward(0, start0, ff0, attn0, mid0b, end0)
    cot[...] = cur[...].astype(BF16)

    @pl.when(swaps)
    def _():
        swap_copy(4, cot, inp_ref).start()

    @pl.when(jnp.logical_not(swaps))
    def _():
        inp_ref[...] = cot[...]

    rs_step(3, 1)
    rs_step(2, 3)
    vec_step(3)
    rs_step(3, 2)
    rs_step(3, 3)
    rs_step(2, 4)
    vec_step(4)
    all_sums = vec_sum[3]
    for i in range(ZS - 1):
        all_sums = all_sums + vec_got[3 + i]
    wide = 2 * d
    per = wide // BLOCKS
    me = ((gi * ZS + z) * 2 + y) * 2 + c
    column = lax.broadcasted_iota(jnp.int32, (HEADS, wide), 1)
    mine = jnp.where(column // per == me, all_sums, 0.0)
    source = lax.broadcasted_iota(jnp.int32, (wide, 128), 0)
    target = lax.broadcasted_iota(jnp.int32, (wide, 128), 1)
    fold = (source % per == target).astype(F32)
    vec_ref[...] = lax.dot_general(
        mine, fold, (((1,), (0,)), ((), ())), preferred_element_type=F32, precision=lax.Precision.HIGHEST
    )
    rs_step(3, 4)

    @pl.when(is_known)
    def _():
        for l in range(2):
            for copy in kv_copies(l):
                copy.wait_send()

    @pl.when(jnp.logical_not(is_known))
    def _():
        for l in range(2):
            for i in range(pairs):
                for copy in dkv_copies(l, i):
                    copy.wait_send()

    @pl.when(swaps)
    def _():
        swap_copy(3, x_in, out_ref).wait()
        swap_copy(4, cot, inp_ref).wait()


def run_kernel(tokens, cotangent, blocks, order, lengths, known, replicas):
    n, d = tokens.shape
    layers = 2
    vmem = pl.BlockSpec(memory_space=pltpu.VMEM)

    def buf(*shape, dtype=BF16):
        return pltpu.VMEM(shape, dtype)

    grid = (2, ZS, 2, 2, 16)
    dma = pltpu.SemaphoreType.DMA
    scratch = [
        buf(MATRICES, *grid, d),
        buf(n, d), buf(n, d),
        buf(8, 2 * n, dtype=F32), buf(8, 2 * n, dtype=F32),
        buf(n, n, dtype=F32),
        buf(n, d, dtype=F32),
        buf(layers, n, d), buf(layers, n, d), buf(layers, n, d), buf(layers, n, d),
        buf(layers, n, d), buf(layers, n, d),
        buf(layers, HEADS, n, n),
        buf(layers, HEADS, n, dtype=F32),
        buf(layers, n, d),
        buf(layers, n, d), buf(layers, n, 1, dtype=F32),
        buf(layers, n, d), buf(layers, n, d, dtype=F32), buf(layers, n, d),
        buf(layers, n, d), buf(layers, n, 1, dtype=F32),
        buf(n, d, dtype=F32), buf(n, d),
        buf(n, d, dtype=F32), buf(n, d, dtype=F32), buf(n, d, dtype=F32),
        buf(layers, n, d), buf(layers, n, d), buf(layers, n, d), buf(layers, n, d),
        buf(12, *grid, d),
        buf(12, 2, ZS, 2, 16, d),
        buf(12, 2, ZS, 16, d // 2), buf(12, ZS, 2, 16, d // 2),
        buf(12, ZS, 16, d), buf(ZS - 1, 12, 16, d),
        buf(4, 8, 2 * d, dtype=F32), buf(6, 8, 2 * d, dtype=F32),
        dma((5,)), dma((5,)),
        dma((len(GATHERS), 8)), dma((len(GATHERS), 8)),
        dma((layers, 2)), dma((layers, 2)),
        dma((layers, d // 128, 2)), dma((layers, d // 128, 2)),
        dma((len(REDUCES), 8)), dma((len(REDUCES), 8)),
        dma((6,)), dma((6,)),
    ]
    return pl.pallas_call(
        functools.partial(kernel, replicas),
        out_shape=(
            jax.ShapeDtypeStruct((n, d), BF16),
            jax.ShapeDtypeStruct((n, d), BF16),
            jax.ShapeDtypeStruct((12, 16, d), F32),
            jax.ShapeDtypeStruct((8, 128), F32),
        ),
        in_specs=[vmem] * 6,
        out_specs=(vmem,) * 4,
        scratch_shapes=scratch,
        compiler_params=pltpu.CompilerParams(
            collective_id=0, has_side_effects=True, vmem_limit_bytes=62 * 2**20
        ),
    )(tokens, cotangent, blocks, order, lengths, known)


def shards(
    tokens, qkv_weight, out_weight, ff_weight, ln_gain, ln_bias, order, cell_lengths, known_mask, cotangent
):
    _, half_len, d = tokens.shape
    dp_size = lax.axis_size("dp")
    replicas = dp_size * 2 // BLOCKS
    groups = [[i * replicas + j for j in range(replicas)] for i in range(dp_size // replicas)]
    rows = d // (2 * dp_size)

    def square(array, layer, *which):
        return array[(layer, *which)].reshape(1, rows, d)

    pieces = []
    for layer in range(2):
        pieces += [square(qkv_weight, layer, 1), square(qkv_weight, layer, 2), square(qkv_weight, layer, 0)]
        pieces += [square(out_weight, layer), square(ff_weight, layer, 0), square(ff_weight, layer, 1)]
    mats = jnp.concatenate(pieces, axis=0)
    vecs = jnp.stack([ln_gain[0], ln_bias[0], ln_gain[1], ln_bias[1]])
    if replicas > 1:
        mats = lax.all_gather(mats, "dp", axis=1, tiled=True, axis_index_groups=groups)
        vecs = lax.all_gather(vecs, "dp", axis=1, tiled=True, axis_index_groups=groups)
    vecs = jnp.pad(vecs.reshape(1, 1, -1), ((0, 0), (0, 15), (0, d - vecs.size)))
    blocks = jnp.concatenate([mats[:6], vecs, mats[6:]], axis=0)
    out, inp, grads, vec = run_kernel(
        tokens[0], cotangent[0], blocks, order, cell_lengths, known_mask, replicas
    )
    per = 2 * d // BLOCKS
    vec = vec[:, :per]
    if replicas > 1:
        grads = lax.psum_scatter(grads, "dp", scatter_dimension=1, tiled=True, axis_index_groups=groups)
        vec = lax.psum_scatter(vec, "dp", scatter_dimension=1, tiled=True, axis_index_groups=groups)
    grads = grads.reshape(2, 6, -1)
    qkv_grad = jnp.stack([grads[:, QUERY], grads[:, KEY], grads[:, VALUE]], axis=1)
    ff_grad = grads[:, UP : DOWN + 1]
    return (
        out.astype(F32)[None],
        inp.astype(F32)[None],
        qkv_grad,
        grads[:, OUT],
        ff_grad,
        vec[0::4],
        vec[1::4],
    )


def solution(mesh):
    flat = ("group", "dp")
    return jax.shard_map(
        shards,
        mesh=mesh,
        in_specs=(
            P("dp", "group", None),
            P(None, None, flat),
            P(None, flat),
            P(None, None, flat),
            P(None, flat),
            P(None, flat),
            P("dp", None),
            P("dp", None),
            P("dp", None),
            P("dp", "group", None),
        ),
        out_specs=(
            P("dp", "group", None),
            P("dp", "group", None),
            P(None, None, flat),
            P(None, flat),
            P(None, None, flat),
            P(None, flat),
            P(None, flat),
        ),
        check_vma=False,
    )
```

time: 678 us -> 131 us (0.19); the launches traced: 670 us -> 131 us
  waiting for transfers between devices: 225 us -> 0 us
  blocking collectives: 171 us -> 0 us
  Pallas kernels: 0 us -> 117 us
  local copies, waits for them, and re-layouts: 124 us -> 9.78 us
  other arithmetic: 62.8 us -> 2.33 us
  matrix products: 57 us -> 0 us
  starting transfers between devices: 14.8 us -> 0 us
  between operations: 15.5 us -> 0.91 us
    unnamed x6 -> x0, waiting for transfers between devices: 210 us -> none
    pallas_call x0 -> x1, Pallas kernels: none -> 117 us  [run_kernel(): pl.pallas_call(functools.partial(kernel, replicas), out_shape=(jax.ShapeD...]
    all_gather x2 -> x0, blocking collectives: 90.9 us -> none  [shards(): lax.all_gather(out_weight[layer_index], ('group', 'dp'), axis=0, tiled=True)]
    unnamed x2 -> x0, blocking collectives: 80.1 us -> none
    slice x12 -> x8, local copies, waits for them, and re-layouts: 65.8 us -> 3.89 us  [the longest x3 1.86 us: square(): return array[layer, *which].reshape(1, rows, d)]
    dot_general x48 -> x0, matrix products: 57 us -> none  [the longest x2 5.74 us: attend_back(): jnp.einsum('qhd,khd->hqk', grad_block, value_rows, preferred_element_type...]
    unnamed x123 -> x30, local copies, waits for them, and re-layouts: 33.5 us -> 4.34 us
    all_gather x2 -> x0, other arithmetic: 21.8 us -> none  [shards(): lax.all_gather(out_weight[layer_index], ('group', 'dp'), axis=0, tiled=True)]
  transfers between devices with their start and end apart: 13 -> 0, of which waited for: 3 -> 0; matrix products, arithmetic and copies ran while one was open for 28% -> 0% of each run, Pallas kernels for 0% -> 0%
where the time goes in v1:
time: 131 us
  Pallas kernels  117 us (89%)
  local copies, waits for them, and re-layouts  9.78 us (7%)
  other arithmetic  2.33 us (2%)
    pallas_call x1, Pallas kernels, run_kernel(): pl.pallas_call(functools.partial(kernel, replicas), out_shape=(jax.ShapeD...  117 us
    unnamed x30, local copies, waits for them, and re-layouts  4.34 us

profile of v1, /device:TPU:0, one launch (start us, length us, event | category | flops | bytes accessed | tf_op | source)
XLA Modules:
  0.0 130.5 jit_solution(5672595897903964338)
XLA Ops:
  0.6 0.0 copy-start.5
  0.6 0.0 copy-start.6
  0.7 0.6 copy-done.5
  1.3 0.0 copy-done.6
  1.3 0.1 reshape.20
  1.4 0.0 copy-start.3
  1.4 1.0 slice_reduce_fusion.2
  2.5 0.0 copy-done.3
  2.5 0.3 slice_reduce_fusion
  2.8 0.0 copy-start.2
  3.0 0.8 copy-done.2
  3.7 0.5 slice_reduce_fusion.3
  4.6 0.0 copy-start.4
  4.6 0.7 copy-done.4
  5.3 117.5 %shard_map.153 = (bf16[512,512]{1,0:T(8,128)(2,1)}, bf16[512,512]{1,0:T(8,128)(2,1)}, f32[12,16,512]{2,1,0:T(8,128)}, f32[8,128]{1,0:T(8,128)}) custom-call(bf16[512,512]{1,0:T(8,128)(2,1)} %bitcast.12, bf16[512,512]{1,0:T(8,128)(2,1)} %bitcast.13, bf16[13,16,512]{2,1,0:T(8,128)(2,1)} %copy-done.4, s32[1,1024]{1,0:T(1,128)} %refs_3_.1, s32[1,3]{1,0:T(1,128)} %refs_4_.1, ...), custom_call_target="tpu_custom_call" | custom-call | tf_op jit(solution)/shard_map/pallas_call | solution.py:638
  122.8 0.0 copy-start.7
  122.8 0.7 copy-done.7
  123.4 0.6 slice.97
  124.0 0.6 slice.96
  124.6 1.2 reshape.21
  125.8 0.1 fusion.1
  125.9 0.8 fusion
  126.7 0.0 copy-start.1
  126.7 0.7 copy.21
  127.4 0.1 pad_maximum_fusion
  127.5 0.8 copy.18
  128.3 0.0 copy-done.1
  128.3 0.0 copy-start
  128.3 1.1 bitcast_convert_fusion.1
  129.4 0.0 copy-done
  129.4 1.1 bitcast_convert_fusion
  (27 shorter events, 0.3 us)
Async XLA Ops:
  0.6 0.7 copy-start.5
  0.6 0.7 copy-start.6
  1.4 1.1 copy-start.3
  2.8 0.9 copy-start.2
  4.6 0.7 copy-start.4
  122.8 0.7 copy-start.7
  126.7 1.6 %copy-start.1 = (bf16[512,512]{1,0:T(8,128)(2,1)S(1)}, bf16[512,512]{1,0:T(8,128)(2,1)}, u32[]{:S(2)}) copy-start(bf16[512,512]{1,0:T(8,128)(2,1)} %get-tuple-element.11) | copy-start | bytes 1572868
  128.3 1.1 copy-start
